TPU v7x, 32 devices: a whole 2x2x4 slice. The times are simulated.
32 devices in a mesh: blk: 8 (over y, x, core), exp: 4 (over z).
Axes of the slice: x: 2, y: 2, z: 4, core: 2. Of those that a mesh axis runs over, the one named last changes fastest.
Arguments:
- residual_deposit_sequence: bfloat16 [4, 1024, 1536], P('exp', 'blk'), may hold values from -60 to 60
- premix_rescaler: float32 [1536], replicated, may hold values from 0.25 to 1.75
- asking_projector: bfloat16 [1536, 1536], P(None, 'exp'), may hold values from -0.15625 to 0.15625
- lookup_projector: bfloat16 [1536, 512], P(None, 'exp'), may hold values from -0.15625 to 0.15625
- content_projector: bfloat16 [1536, 512], P(None, 'exp'), may hold values from -0.15625 to 0.15625
- final_projector: bfloat16 [1536, 1536], P('exp'), may hold values from -0.15625 to 0.15625
- logit_multipliers: float32 [12], replicated, may hold values from 1.5 to 6
- premixture_rescaler: float32 [1536], replicated, may hold values from 0.25 to 1.75
- specialist_switch_tensor: bfloat16 [8, 1536, 384], P('exp'), may hold values from -0.15625 to 0.15625
- specialist_widen_tensor: bfloat16 [8, 1536, 384], P('exp'), may hold values from -0.15625 to 0.15625
- specialist_shrink_tensor: bfloat16 [8, 384, 1536], P('exp'), may hold values from -0.3125 to 0.3125
- picked_specialist_labels: int32 [4, 1024, 2], P(None, 'blk'), may hold values from 0 to 7, all different within a row; in each aligned block of 128 rows (0 to 127, 128 to 255, ..., all dimensions but the last counted through in order) at most 64 rows name the same one
- specialist_shares: float32 [4, 1024, 2], P(None, 'blk'), may hold values from 0.1 to 1
Outputs:
- attention_update: bfloat16 [4, 1024, 1536], P('exp', 'blk')
- expert_update: bfloat16 [4, 1024, 1536], P('exp', 'blk')
Inputs may be any that keep to these rules, and one draw needn't show every extreme that they name: `picked_specialist_labels`: the 2 ids of a hit differ. Within each event's 128 hits on one index of blk (an aligned block of 128 rows) no expert is named by more than 64 hits, a bound that some block reaches.
All inputs are finite; a program needn't handle non-finite values.
Results may differ from a plain program's by a relative error of at most 0.019.
Values may be sent and summed in bfloat16 or wider, within the bound.
A program may use at most 192 MiB of HBM per device.

v0:
```python
import math
import jax
import jax.numpy as jnp
from jax import lax
from jax.sharding import PartitionSpec as P

D = 1536
PER_LANE_DIM = 128
TOP = 2
CAP = 64


def norm_rows(values, norm_gain):
    widened = values.astype(jnp.float32)
    return (
        widened * lax.rsqrt(jnp.mean(widened * widened, axis=-1, keepdims=True) + 1e-05) * norm_gain
    )


def head_norm(values):
    return values * lax.rsqrt(jnp.mean(values * values, axis=-1, keepdims=True) + 1e-06)


def attend_hits(
    rescaled_entries,
    asking_projector,
    lookup_projector,
    content_projector,
    final_projector,
    logit_multipliers,
):
    events, row_count, model_width = rescaled_entries.shape
    common_key_heads = lookup_projector.shape[1] // PER_LANE_DIM
    local_lane_count = asking_projector.shape[1] // PER_LANE_DIM
    askers_per_lookup = local_lane_count // common_key_heads
    query_heads = jnp.einsum(
        "std,de->ste", rescaled_entries, asking_projector, preferred_element_type=jnp.float32
    )
    query_heads = head_norm(
        query_heads.reshape(events, row_count, common_key_heads, askers_per_lookup, PER_LANE_DIM)
    ).astype(jnp.bfloat16)
    key_heads = jnp.einsum(
        "std,de->ste", rescaled_entries, lookup_projector, preferred_element_type=jnp.float32
    )
    key_heads = head_norm(
        key_heads.reshape(events, row_count, common_key_heads, PER_LANE_DIM)
    ).astype(jnp.bfloat16)
    value_heads = jnp.einsum(
        "std,de->ste", rescaled_entries, content_projector, preferred_element_type=jnp.float32
    )
    value_heads = value_heads.reshape(events, row_count, common_key_heads, PER_LANE_DIM).astype(
        jnp.bfloat16
    )
    inverse_root_dim = (logit_multipliers / math.sqrt(PER_LANE_DIM)).reshape(
        common_key_heads, askers_per_lookup
    )
    key_piece = lax.all_gather(key_heads, "blk", axis=1, tiled=True)
    value_piece = lax.all_gather(value_heads, "blk", axis=1, tiled=True)
    scores = jnp.einsum(
        "sikgd,sjkd->skgij", query_heads, key_piece, preferred_element_type=jnp.float32
    )
    expo = jnp.exp(scores * inverse_root_dim[None, :, :, None, None])
    totals = jnp.sum(expo, axis=-1)
    mixture = jnp.einsum(
        "skgij,sjkd->skgid",
        expo.astype(jnp.bfloat16),
        value_piece,
        preferred_element_type=jnp.float32,
    )
    totals, mixture = (totals, mixture)
    heads_out = head_norm(mixture / totals[..., None]).astype(jnp.bfloat16)
    out_blocks = final_projector.reshape(
        common_key_heads, askers_per_lookup, PER_LANE_DIM, model_width
    )
    return jnp.einsum("skgid,kgde->sie", heads_out, out_blocks, preferred_element_type=jnp.float32)


def gates_of(labels, shares, expert_ids):
    hit = labels[..., None, :] == expert_ids[:, None]
    return jnp.sum(jnp.where(hit, shares[..., None, :], 0.0), axis=-1)


def run_experts(rows, gates, switch, widen, shrink):
    gate_act = jnp.einsum("td,jdf->tjf", rows, switch, preferred_element_type=jnp.float32)
    up_act = jnp.einsum("td,jdf->tjf", rows, widen, preferred_element_type=jnp.float32)
    hidden = (jax.nn.silu(gate_act) * up_act * gates[:, :, None]).astype(jnp.bfloat16)
    return jnp.einsum("tjf,jfd->td", hidden, shrink, preferred_element_type=jnp.float32)


def body(
    residual_deposit_sequence,
    premix_rescaler,
    asking_projector,
    lookup_projector,
    content_projector,
    final_projector,
    logit_multipliers,
    premixture_rescaler,
    specialist_switch_tensor,
    specialist_widen_tensor,
    specialist_shrink_tensor,
    picked_specialist_labels,
    specialist_shares,
):
    specialist_slot = lax.axis_index("exp")
    exp_count = lax.axis_size("exp")
    rows_all = lax.all_gather(residual_deposit_sequence, "exp", axis=0, tiled=True)
    rescaled_entries = norm_rows(rows_all, premix_rescaler).astype(jnp.bfloat16)
    local_lane_count = asking_projector.shape[1] // PER_LANE_DIM
    device_scratch = lax.dynamic_slice_in_dim(
        logit_multipliers, specialist_slot * local_lane_count, local_lane_count
    )
    partial_out = attend_hits(
        rescaled_entries,
        asking_projector,
        lookup_projector,
        content_projector,
        final_projector,
        device_scratch,
    )
    attention_full = lax.psum_scatter(
        partial_out.astype(jnp.bfloat16), "exp", scatter_dimension=0, tiled=True
    ).astype(jnp.float32)
    attention_update = attention_full.astype(jnp.bfloat16)
    residual = residual_deposit_sequence.astype(jnp.float32) + attention_full
    expert_in = norm_rows(residual, premixture_rescaler).astype(jnp.bfloat16)
    local_experts = specialist_switch_tensor.shape[0]
    expert_ids = specialist_slot * local_experts + jnp.arange(local_experts, dtype=jnp.int32)
    gates = gates_of(picked_specialist_labels, specialist_shares, expert_ids)
    rows = lax.all_gather(expert_in, "exp", axis=0, tiled=True)
    events, row_count, _ = rows.shape
    summed = run_experts(
        rows.reshape(events * row_count, D),
        gates.reshape(events * row_count, local_experts),
        specialist_switch_tensor,
        specialist_widen_tensor,
        specialist_shrink_tensor,
    ).astype(jnp.bfloat16)
    expert_update = lax.psum_scatter(
        summed.reshape(events, row_count, D), "exp", scatter_dimension=0, tiled=True
    )
    return (attention_update, expert_update)


def solution(mesh):
    placed = (
        P("exp", "blk", None),
        P(),
        P(None, "exp"),
        P(None, "exp"),
        P(None, "exp"),
        P("exp", None),
        P(),
        P(),
        P("exp", None, None),
        P("exp", None, None),
        P("exp", None, None),
        P(None, "blk", None),
        P(None, "blk", None),
    )
    return jax.shard_map(
        body,
        mesh=mesh,
        in_specs=placed,
        out_specs=(P("exp", "blk", None), P("exp", "blk", None)),
        check_vma=False,
    )
```

profile of v0, /device:TPU:0, one launch (start us, length us, event | category | flops | bytes accessed | tf_op | source)
XLA Modules:
  0.0 236.5 jit_solution(15688548943295369664)
XLA Ops:
  7.2 0.0 all-gather.7.cloned.1.call-start
  7.2 0.7 all-gather.7.cloned.1.call-update
  7.9 0.0 all-gather.11.cloned.1.call-start
  8.0 41.4 %all-gather.7.cloned.1.call-done = bf16[4,128,1536]{2,1,0:T(8,128)(2,1)} async-done(((bf16[1,128,1536]{2,1,0:T(8,128)(2,1)}), bf16[4,128,1536]{2,1,0:T(8,128)(2,1)}) %all-gather.7.cloned.1.call-update) | async-done | bytes 1572880 | tf_op jit(solution)/shard_map/all_gather | solution.py:107
  49.4 1.9 fusion.1
  51.4 1.5 multiply_reduce_fusion.2
  52.9 0.7 multiply_convert_fusion.6
  53.6 0.0 all-gather.11.cloned.1.call-update
  53.6 0.0 all-gather.13.cloned.1.call-start
  53.7 2.7 %convolution_convert_fusion = bf16[4,128,128]{2,1,0:T(8,128)(2,1)} fusion(bf16[4,128,1536]{2,1,0:T(8,128)(2,1)} %all-gather.7.cloned.1.call-done, f32[1536]{0:T(1024)S(1)} %copy-done.9, f32[4,128]{1,0:T(4,128)S(1)} %add_rsqrt_fusion.3, bf16[1536,128]{1,0:T(8,128)(2,1)S(1)} %copy-done.8), kind=kOutput, calls=%fused_computation.19 | convolution fusion | flops 204537856 | bytes 2105344 | tf_op jit(solution)/shard_map/std,de->ste/dot_general | solution.py:48
  56.4 0.0 all-gather.13.cloned.1.call-update
  56.4 0.0 reduce-scatter.3.cloned.1.call-start
  56.5 0.1 dynamic-slice_multiply_fusion
  56.6 3.7 %fusion.31 = (f32[4,128,384]{2,1,0:T(8,128)S(1)}, f32[4,128,384]{2,1,0:T(8,128)}) fusion(bf16[1536,384]{1,0:T(8,128)(2,1)} %param.15, bf16[4,128,1536]{2,1,0:T(8,128)(2,1)} %all-gather.7.cloned.1.call-done, f32[1536]{0:T(1024)S(1)} %copy-done.9, f32[4,128]{1,0:T(4,128)S(1)} %add_rsqrt_fusion.3), kind=kOutput, calls=%fused_computation.49 | convolution fusion | flops 607322112 | bytes 4333568 | tf_op jit(solution)/shard_map/std,de->ste/dot_general | solution.py:36
  60.2 1.2 copy.43
  61.4 1.4 copy.42
  62.8 1.2 reduce_sum.65
  64.0 12.2 %all-gather.11.cloned.1.call-done = bf16[4,1024,128]{1,2,0:T(8,128)(2,1)} async-done(((bf16[4,128,128]{1,2,0:T(8,128)(2,1)}), bf16[4,1024,128]{1,2,0:T(8,128)(2,1)}) %all-gather.11.cloned.1.call-update) | async-done | bytes 1048592 | tf_op jit(solution)/shard_map/all_gather | solution.py:57
  76.2 5.4 %bitcast_reduce_fusion = (f32[4,3,128]{2,1,0:T(4,128)S(1)}, f32[4,1024,128,3]{2,1,3,0:T(8,128)}) fusion(f32[3]{0:T(128)S(1)} %dynamic-slice_multiply_fusion, f32[4,128,3,128]{1,3,2,0:T(8,128)S(1)} %bitcast.91, f32[4,128,3]{1,2,0:T(4,128)S(1)} %add_rsqrt_fusion.1, bf16[4,1024,128]{1,2,0:T(8,128)(2,1)} %all-gather.11.cloned.1.call-done), kind=kOutput, calls=%fused_computation | convolution fusion | flops 406190592 | bytes 8138764 | tf_op jit(solution)/shard_map/sikgd,sjkd->skgij/dot_general | solution.py:59
  81.6 20.6 %all-gather.13.cloned.1.call-done = bf16[4,1024,128]{2,1,0:T(8,128)(2,1)} async-done(((bf16[4,128,128]{2,1,0:T(8,128)(2,1)}), bf16[4,1024,128]{2,1,0:T(8,128)(2,1)}) %all-gather.13.cloned.1.call-update) | async-done | bytes 1048592 | tf_op jit(solution)/shard_map/all_gather | solution.py:58
  102.2 4.4 %multiply_reduce_fusion.1 = (f32[4,3,128]{2,1,0:T(4,128)S(1)}, f32[4,3,128,128]{2,3,1,0:T(8,128)S(1)}) fusion(f32[4,3,128]{2,1,0:T(4,128)S(1)} %get-tuple-element.6, bf16[4,1024,128]{2,1,0:T(8,128)(2,1)} %all-gather.13.cloned.1.call-done, f32[4,1024,128,3]{2,1,3,0:T(8,128)} %get-tuple-element.7, f32[3]{0:T(128)S(1)} %dynamic-slice_multiply_fusion), kind=kOutput, calls=%fused_computation.31 | convolution fusion | flops 406387200 | bytes 8138764 | tf_op jit(solution)/shard_map/skgij,sjkd->skgid/dot_general | solution.py:64
  106.7 2.2 fusion.8
  108.9 0.0 all-gather.9.cloned.1.call-start
  109.0 35.4 %reduce-scatter.3.cloned.1.call-done = bf16[1,128,1536]{2,1,0:T(8,128)(2,1)} async-done(((bf16[4,128,1536]{2,1,0:T(8,128)(2,1)}), bf16[1,128,1536]{2,1,0:T(8,128)(2,1)}) %reduce-scatter.3.cloned.1.call-update) | async-done | bytes 393232 | tf_op jit(solution)/shard_map/reduce_scatter | solution.py:121
  144.4 1.2 multiply_reduce_fusion
  145.6 1.9 multiply_convert_fusion.1
  147.5 0.0 reduce-scatter.5.cloned.1.call-start
  147.6 0.1 select_reduce_fusion
  147.7 36.0 %all-gather.9.cloned.1.call-done = bf16[4,128,1536]{2,1,0:T(8,128)(2,1)} async-done(((bf16[1,128,1536]{2,1,0:T(8,128)(2,1)}), bf16[4,128,1536]{2,1,0:T(8,128)(2,1)}) %all-gather.9.cloned.1.call-update) | async-done | bytes 1572880 | tf_op jit(solution)/shard_map/all_gather | solution.py:130
  183.7 4.7 %fusion.32 = f32[512,2,384]{2,0,1:T(8,128)} fusion(bf16[512,1536,1]{1,0,2:T(8,128)(2,1)} %bitcast.97, bf16[2,1536,384]{2,1,0:T(8,128)(2,1)} %param.21), kind=kOutput, calls=%fused_computation.50 | convolution fusion | flops 1207959552 | bytes 5505024 | tf_op jit(solution)/shard_map/td,jdf->tjf/dot_general | solution.py:84
  188.4 6.9 %fusion.9 = bf16[512,1536]{1,0:T(8,128)(2,1)} fusion(bf16[2,384,1536]{2,1,0:T(8,128)(2,1)S(1)} %copy-done, f32[512,2,384]{2,0,1:T(8,128)} %fusion.32, bf16[512,1536,1]{1,0,2:T(8,128)(2,1)} %bitcast.98, bf16[2,1536,384]{2,1,0:T(8,128)(2,1)} %param.22, f32[512,2]{0,1:T(2,128)S(1)} %bitcast.96), kind=kOutput, calls=%fused_computation.15 | convolution fusion | flops 2419458048 | bytes 9441280 | tf_op jit(solution)/shard_map/tjf,jfd->td/dot_general | solution.py:87
  195.3 34.3 %reduce-scatter.5.cloned.1.call-done = bf16[1,128,1536]{2,1,0:T(8,128)(2,1)} async-done(((bf16[4,128,1536]{2,1,0:T(8,128)(2,1)}), bf16[1,128,1536]{2,1,0:T(8,128)(2,1)}) %reduce-scatter.5.cloned.1.call-update) | async-done | bytes 393232 | tf_op jit(solution)/shard_map/reduce_scatter | solution.py:139
  (34 shorter events, 0.2 us)
Async XLA Ops:
  7.2 181.2 %copy-start = (bf16[2,384,1536]{2,1,0:T(8,128)(2,1)S(1)}, bf16[2,384,1536]{2,1,0:T(8,128)(2,1)}, u32[]{:S(2)}) copy-start(bf16[2,384,1536]{2,1,0:T(8,128)(2,1)} %param.23) | copy-start | bytes 7077892
  7.2 44.2 %copy-start.7 = (bf16[1536,128]{1,0:T(8,128)(2,1)S(1)}, bf16[1536,128]{1,0:T(8,128)(2,1)}, u32[]{:S(2)}) copy-start(bf16[1536,128]{1,0:T(8,128)(2,1)} %param.16) | copy-start | bytes 1179652
  7.2 42.2 %all-gather.7.cloned.1.call-start = ((), (), s32[]{:S(2)}) async-start(), calls=%async_computation.2 | async-start | bytes 1966080 | tf_op jit(solution)/shard_map/all_gather | solution.py:107
  7.9 68.3 %all-gather.11.cloned.1.call-start = ((), (), s32[]{:S(2)}) async-start(), calls=%async_computation.6 | async-start | bytes 1179648 | tf_op jit(solution)/shard_map/all_gather | solution.py:57
  49.4 1.9 copy-start.2
  51.4 2.3 copy-start.8
  51.4 2.3 copy-start.9
  53.6 2.9 %copy-start.10 = (f32[12]{0:T(128)S(1)}, f32[12]{0:T(128)}, u32[]{:S(2)}) copy-start(f32[12]{0:T(128)} %param.19) | copy-start | bytes 148
  53.6 48.6 %all-gather.13.cloned.1.call-start = ((), (), s32[]{:S(2)}) async-start(), calls=%async_computation.7 | async-start | bytes 1179648 | tf_op jit(solution)/shard_map/all_gather | solution.py:58
  56.4 87.9 %reduce-scatter.3.cloned.1.call-start = ((), (), s32[]{:S(2)}) async-start(), calls=%async_computation.3 | async-start | bytes 1966080 | tf_op jit(solution)/shard_map/reduce_scatter | solution.py:121
  102.2 4.5 %copy-start.3 = (bf16[384,1536]{1,0:T(8,128)(2,1)S(1)}, bf16[384,1536]{1,0:T(8,128)(2,1)}, u32[]{:S(2)}) copy-start(bf16[384,1536]{1,0:T(8,128)(2,1)} %param.18) | copy-start | bytes 3538948
  108.9 35.5 %copy-start.1 = (bf16[1,128,1536]{2,1,0:T(8,128)(2,1)S(1)}, bf16[1,128,1536]{2,1,0:T(8,128)(2,1)}, u32[]{:S(2)}) copy-start(bf16[1,128,1536]{2,1,0:T(8,128)(2,1)} %param.13) | copy-start | bytes 1179652
  108.9 36.7 %copy-start.4 = (f32[1536]{0:T(1024)S(1)}, f32[1536]{0:T(1024)}, u32[]{:S(2)}) copy-start(f32[1536]{0:T(1024)} %param.20) | copy-start | bytes 18436
  108.9 38.6 %copy-start.5 = (s32[4,128,2]{1,2,0:T(2,128)S(1)}, s32[4,128,2]{1,2,0:T(2,128)}, u32[]{:S(2)}) copy-start(s32[4,128,2]{1,2,0:T(2,128)} %param.24) | copy-start | bytes 12292
  108.9 38.7 %copy-start.6 = (f32[4,128,2]{1,2,0:T(2,128)S(1)}, f32[4,128,2]{1,2,0:T(2,128)}, u32[]{:S(2)}) copy-start(f32[4,128,2]{1,2,0:T(2,128)} %param.25) | copy-start | bytes 12292
  108.9 74.8 %all-gather.9.cloned.1.call-start = ((), (), s32[]{:S(2)}) async-start(), calls=%async_computation.4 | async-start | bytes 1966080 | tf_op jit(solution)/shard_map/all_gather | solution.py:130
  147.5 82.1 %reduce-scatter.5.cloned.1.call-start = ((), (), s32[]{:S(2)}) async-start(), calls=%async_computation.5 | async-start | bytes 1966080 | tf_op jit(solution)/shard_map/reduce_scatter | solution.py:139
Sparse Core Ops, SparseCore 0:
  9.6 39.7 all-gather.6
  53.8 22.4 all-gather.10
  78.7 23.4 all-gather.12
  109.0 35.2 reduce-scatter.2
  147.6 36.0 all-gather.8
  195.4 34.1 reduce-scatter.4
where the time goes:
time: 237 us; the launch traced here: 236 us
  waiting for transfers between devices  181 us (76%)
  matrix products  31.5 us (13%)
  between operations  14.3 us (6%)
  other arithmetic  7.1 us (3%)
  local copies, waits for them, and re-layouts  2.62 us (1%)
    all_gather x1, waiting for transfers between devices, body(): lax.all_gather(residual_deposit_sequence, 'exp', axis=0, tiled=True)  41.4 us
    all_gather x1, waiting for transfers between devices, body(): rows = lax.all_gather(expert_in, 'exp', axis=0, tiled=True)  36 us
    reduce_scatter x1, waiting for transfers between devices, body(): lax.psum_scatter(partial_out.astype(jnp.bfloat16), 'exp', scatter_dimensi...  35.4 us
    reduce_scatter x1, waiting for transfers between devices, body(): lax.psum_scatter(summed.reshape(events, row_count, D), 'exp', scatter_dim...  34.3 us
    all_gather x1, waiting for transfers between devices, attend_hits(): value_piece = lax.all_gather(value_heads, 'blk', axis=1, tiled=True)  20.6 us
    all_gather x1, waiting for transfers between devices, attend_hits(): key_piece = lax.all_gather(key_heads, 'blk', axis=1, tiled=True)  12.2 us
    dot_general x1, matrix products, run_experts(): jnp.einsum('tjf,jfd->td', hidden, shrink, preferred_element_type=jnp.floa...  6.9 us
    dot_general x1, matrix products, attend_hits(): jnp.einsum('sikgd,sjkd->skgij', query_heads, key_piece, preferred_element...  5.4 us
  transfers between devices with their start and end apart: 6, of which 6 were waited for; matrix products, arithmetic and copies ran while one was open for 7% of the time, Pallas kernels for 0%

commit v1 on v0

--- a/solution.py
+++ b/solution.py
@@ -8,6 +8,18 @@
 PER_LANE_DIM = 128
 TOP = 2
 CAP = 64
+
+
+def gather_around(value, axis, dim):
+    ways, here, turn = (lax.axis_size(axis), lax.axis_index(axis), value.shape[dim])
+    lengths = [n * ways if d == dim else n for d, n in enumerate(value.shape)]
+    full = lax.dynamic_update_slice_in_dim(
+        jnp.zeros(lengths, value.dtype), value, here * turn, axis=dim
+    )
+    for far in range(1, ways):
+        value = lax.ppermute(value, axis, [(d, (d + 1) % ways) for d in range(ways)])
+        full = lax.dynamic_update_slice_in_dim(full, value, (here - far) % ways * turn, axis=dim)
+    return full
 
 
 def norm_rows(values, norm_gain):
@@ -55,7 +67,7 @@
         common_key_heads, askers_per_lookup
     )
     key_piece = lax.all_gather(key_heads, "blk", axis=1, tiled=True)
-    value_piece = lax.all_gather(value_heads, "blk", axis=1, tiled=True)
+    value_piece = gather_around(value_heads, "blk", 1)
     scores = jnp.einsum(
         "sikgd,sjkd->skgij", query_heads, key_piece, preferred_element_type=jnp.float32
     )

time: 237 us -> 229 us (0.966)
  waiting for transfers between devices: 181 us -> 168 us
  local copies, waits for them, and re-layouts: 2.62 us -> 13.2 us
  matrix products: 31.5 us -> 26.9 us
    ppermute x0 -> x7, waiting for transfers between devices: none -> 21.3 us  [gather_around(): lax.ppermute(value, axis, [(d, (d + 1) % ways) for d in range(ways)])]
    all_gather x1 -> x0, waiting for transfers between devices: 20.6 us -> none  [attend_hits(): value_piece = lax.all_gather(value_heads, 'blk', axis=1, tiled=True)]
    all_gather x1, waiting for transfers between devices: 12.2 us -> 0.01 us  [attend_hits(): key_piece = lax.all_gather(key_heads, 'blk', axis=1, tiled=True)]
    dynamic_update_slice x0 -> x8, local copies, waits for them, and re-layouts: none -> 5.47 us  [the longest x7 4.81 us: gather_around(): lax.dynamic_update_slice_in_dim(full, value, (here - far) % ways * turn,...]
    another operation x0 -> x8, local copies, waits for them, and re-layouts: none -> 3.8 us
    dot_general x1, matrix products: 5.4 us -> 2.83 us  [attend_hits(): jnp.einsum('sikgd,sjkd->skgij', query_heads, key_piece, preferred_element...]
  transfers between devices with their start and end apart: 6 -> 12, of which waited for: 6 -> 10; matrix products, arithmetic and copies ran while one was open for 7% -> 8% of each run, Pallas kernels for 0% -> 0%
where the time goes in v1:
time: 229 us
  waiting for transfers between devices  168 us (73%)
  matrix products  26.9 us (12%)
  between operations  14.1 us (6%)
  local copies, waits for them, and re-layouts  13.2 us (6%)
  other arithmetic  5.97 us (3%)
    all_gather x1, waiting for transfers between devices, body(): lax.all_gather(residual_deposit_sequence, 'exp', axis=0, tiled=True)  41.4 us
    all_gather x1, waiting for transfers between devices, body(): rows = lax.all_gather(expert_in, 'exp', axis=0, tiled=True)  35.8 us
    reduce_scatter x1, waiting for transfers between devices, body(): lax.psum_scatter(partial_out.astype(jnp.bfloat16), 'exp', scatter_dimensi...  34.5 us
    reduce_scatter x1, waiting for transfers between devices, body(): lax.psum_scatter(summed.reshape(events, row_count, D), 'exp', scatter_dim...  34.3 us
    ppermute x7, waiting for transfers between devices, gather_around(): lax.ppermute(value, axis, [(d, (d + 1) % ways) for d in range(ways)])  21.3 us
    dot_general x1, matrix products, run_experts(): jnp.einsum('tjf,jfd->td', hidden, shrink, preferred_element_type=jnp.floa...  6.9 us
    dynamic_update_slice x7, local copies, waits for them, and re-layouts, gather_around(): lax.dynamic_update_slice_in_dim(full, value, (here - far) % ways * turn,...  4.81 us
    dot_general x1, matrix products, run_experts(): jnp.einsum('td,jdf->tjf', rows, switch, preferred_element_type=jnp.float32)  4.68 us
  transfers between devices with their start and end apart: 12, of which 10 were waited for; matrix products, arithmetic and copies ran while one was open for 8% of the time, Pallas kernels for 0%

profile of v1, /device:TPU:0, one launch (start us, length us, event | category | flops | bytes accessed | tf_op | source)
XLA Modules:
  0.0 228.7 jit_solution(11958523645760159860)
XLA Ops:
  8.0 41.4 %all-gather.5.cloned.1.call-done = bf16[4,128,1536]{2,1,0:T(8,128)(2,1)} async-done(((bf16[1,128,1536]{2,1,0:T(8,128)(2,1)}), bf16[4,128,1536]{2,1,0:T(8,128)(2,1)}) %all-gather.5.cloned.1.call-update) | async-done | bytes 1572880 | tf_op jit(solution)/shard_map/all_gather | solution.py:119
  49.4 1.9 fusion.1
  51.4 1.5 multiply_reduce_fusion.2
  52.9 0.7 multiply_convert_fusion.6
  53.7 2.0 convolution_convert_fusion
  55.8 5.3 %collective-permute-done = bf16[4,128,1,128]{3,1,0,2:T(8,128)(2,1)S(1)} collective-permute-done((bf16[4,128,1,128]{3,1,0,2:T(8,128)(2,1)S(1)}, bf16[4,128,1,128]{3,1,0,2:T(8,128)(2,1)S(1)}, u32[]{:S(2)}, u32[]{:S(2)}) %collective-permute-start) | collective-permute-done | bytes 131104 | tf_op jit(solution)/shard_map/ppermute | solution.py:20
  61.2 5.2 %collective-permute-done.1 = bf16[4,128,1,128]{3,1,0,2:T(8,128)(2,1)S(1)} collective-permute-done((bf16[4,128,1,128]{3,1,0,2:T(8,128)(2,1)S(1)}, bf16[4,128,1,128]{3,1,0,2:T(8,128)(2,1)S(1)}, u32[]{:S(2)}, u32[]{:S(2)}) %collective-permute-start.1) | collective-permute-done | bytes 131104 | tf_op jit(solution)/shard_map/ppermute | solution.py:20
  66.4 3.9 %fusion.31 = (f32[4,128,384]{2,1,0:T(8,128)}, f32[4,128,384]{2,1,0:T(8,128)}) fusion(bf16[1536,384]{1,0:T(8,128)(2,1)} %param.15, bf16[4,128,1536]{2,1,0:T(8,128)(2,1)} %all-gather.5.cloned.1.call-done, f32[1536]{0:T(1024)S(1)} %copy-done.10, f32[4,128]{1,0:T(4,128)S(1)} %add_rsqrt_fusion.3), kind=kOutput, calls=%fused_computation.57 | convolution fusion | flops 607322112 | bytes 4333568 | tf_op jit(solution)/shard_map/std,de->ste/dot_general | solution.py:48
  70.4 1.4 copy.66
  71.9 1.0 copy.69
  72.9 1.4 copy.65
  74.3 1.1 broadcast.97
  76.2 1.3 collective-permute-done.3
  78.4 0.7 constant_dynamic-update-slice_fusion.5
  79.1 1.0 copy.72
  80.1 3.0 %collective-permute-done.4 = bf16[4,128,1,128]{3,1,0,2:T(8,128)(2,1)S(1)} collective-permute-done((bf16[4,128,1,128]{3,1,0,2:T(8,128)(2,1)}, bf16[4,128,1,128]{3,1,0,2:T(8,128)(2,1)S(1)}, u32[]{:S(2)}, u32[]{:S(2)}) %collective-permute-start.4) | collective-permute-done | bytes 131104 | tf_op jit(solution)/shard_map/ppermute | solution.py:20
  83.8 1.0 copy.73
  84.8 0.7 constant_dynamic-update-slice_fusion.3
  85.6 2.7 %collective-permute-done.5 = bf16[4,128,1,128]{3,1,0,2:T(8,128)(2,1)S(1)} collective-permute-done((bf16[4,128,1,128]{3,1,0,2:T(8,128)(2,1)S(1)}, bf16[4,128,1,128]{3,1,0,2:T(8,128)(2,1)S(1)}, u32[]{:S(2)}, u32[]{:S(2)}) %collective-permute-start.5) | collective-permute-done | bytes 131104 | tf_op jit(solution)/shard_map/ppermute | solution.py:20
  89.2 0.7 constant_dynamic-update-slice_fusion.1
  89.9 3.8 %collective-permute-done.6 = bf16[4,128,1,128]{3,1,0,2:T(8,128)(2,1)S(1)} collective-permute-done((bf16[4,128,1,128]{3,1,0,2:T(8,128)(2,1)S(1)}, bf16[4,128,1,128]{3,1,0,2:T(8,128)(2,1)S(1)}, u32[]{:S(2)}, u32[]{:S(2)}) %collective-permute-start.6) | collective-permute-done | bytes 131104 | tf_op jit(solution)/shard_map/ppermute | solution.py:20
  93.8 0.7 constant_dynamic-update-slice_fusion
  94.5 2.8 %bitcast_reduce_fusion = (f32[4,3,128]{2,1,0:T(4,128)S(1)}, f32[4,1024,128,3]{2,1,3,0:T(8,128)S(1)}) fusion(f32[3]{0:T(128)S(1)} %dynamic-slice_multiply_fusion, f32[4,128,3,128]{1,3,2,0:T(8,128)S(1)} %bitcast.99, f32[4,128,3]{1,2,0:T(4,128)S(1)} %add_rsqrt_fusion.1, bf16[4,1024,128]{1,2,0:T(8,128)(2,1)} %all-gather.9.cloned.1.call-done), kind=kOutput, calls=%fused_computation | convolution fusion | flops 406190592 | bytes 8138764 | tf_op jit(solution)/shard_map/sikgd,sjkd->skgij/dot_general | solution.py:71
  97.4 2.8 %multiply_reduce_fusion.1 = (f32[4,3,128]{2,1,0:T(4,128)S(1)}, f32[4,3,128,128]{2,3,1,0:T(8,128)S(1)}) fusion(f32[4,3,128]{2,1,0:T(4,128)S(1)} %get-tuple-element.6, f32[4,1024,128,3]{2,1,3,0:T(8,128)S(1)} %get-tuple-element.7, f32[3]{0:T(128)S(1)} %dynamic-slice_multiply_fusion, bf16[4,1024,128]{1,2,0:T(8,128)(2,1)} %constant_dynamic-update-slice_fusion), kind=kOutput, calls=%fused_computation.31 | convolution fusion | flops 406387200 | bytes 8138764 | tf_op jit(solution)/shard_map/skgij,sjkd->skgid/dot_general | solution.py:76
  100.2 2.2 fusion.8
  102.4 34.5 %reduce-scatter.3.cloned.1.call-done = bf16[1,128,1536]{2,1,0:T(8,128)(2,1)} async-done(((bf16[4,128,1536]{2,1,0:T(8,128)(2,1)}), bf16[1,128,1536]{2,1,0:T(8,128)(2,1)}) %reduce-scatter.3.cloned.1.call-update) | async-done | bytes 393232 | tf_op jit(solution)/shard_map/reduce_scatter | solution.py:133
  136.9 1.2 multiply_reduce_fusion
  138.1 1.9 multiply_convert_fusion.1
  140.4 35.8 %all-gather.7.cloned.1.call-done = bf16[4,128,1536]{2,1,0:T(8,128)(2,1)} async-done(((bf16[1,128,1536]{2,1,0:T(8,128)(2,1)}), bf16[4,128,1536]{2,1,0:T(8,128)(2,1)}) %all-gather.7.cloned.1.call-update) | async-done | bytes 1572880 | tf_op jit(solution)/shard_map/all_gather | solution.py:142
  176.3 4.7 %fusion.32 = f32[512,2,384]{2,0,1:T(8,128)} fusion(bf16[512,1536,1]{1,0,2:T(8,128)(2,1)} %bitcast.111, bf16[2,1536,384]{2,1,0:T(8,128)(2,1)} %param.21), kind=kOutput, calls=%fused_computation.58 | convolution fusion | flops 1207959552 | bytes 5505024 | tf_op jit(solution)/shard_map/td,jdf->tjf/dot_general | solution.py:96
  180.9 6.9 %fusion.9 = bf16[512,1536]{1,0:T(8,128)(2,1)} fusion(bf16[2,384,1536]{2,1,0:T(8,128)(2,1)S(1)} %copy-done, f32[512,2,384]{2,0,1:T(8,128)} %fusion.32, bf16[512,1536,1]{1,0,2:T(8,128)(2,1)} %bitcast.112, bf16[2,1536,384]{2,1,0:T(8,128)(2,1)} %param.22, f32[512,2]{0,1:T(2,128)S(1)} %bitcast.110), kind=kOutput, calls=%fused_computation.15 | convolution fusion | flops 2419458048 | bytes 9441280 | tf_op jit(solution)/shard_map/tjf,jfd->td/dot_general | solution.py:99
  187.9 34.3 %reduce-scatter.5.cloned.1.call-done = bf16[1,128,1536]{2,1,0:T(8,128)(2,1)} async-done(((bf16[4,128,1536]{2,1,0:T(8,128)(2,1)}), bf16[1,128,1536]{2,1,0:T(8,128)(2,1)}) %reduce-scatter.5.cloned.1.call-update) | async-done | bytes 393232 | tf_op jit(solution)/shard_map/reduce_scatter | solution.py:151
  (64 shorter events, 4.9 us)
Async XLA Ops:
  7.2 173.8 %copy-start = (bf16[2,384,1536]{2,1,0:T(8,128)(2,1)S(1)}, bf16[2,384,1536]{2,1,0:T(8,128)(2,1)}, u32[]{:S(2)}) copy-start(bf16[2,384,1536]{2,1,0:T(8,128)(2,1)} %param.23) | copy-start | bytes 7077892
  7.2 44.2 %copy-start.8 = (bf16[1536,128]{1,0:T(8,128)(2,1)S(1)}, bf16[1536,128]{1,0:T(8,128)(2,1)}, u32[]{:S(2)}) copy-start(bf16[1536,128]{1,0:T(8,128)(2,1)} %param.16) | copy-start | bytes 1179652
  7.2 42.2 %all-gather.5.cloned.1.call-start = ((), (), s32[]{:S(2)}) async-start(), calls=%async_computation.2 | async-start | bytes 1966080 | tf_op jit(solution)/shard_map/all_gather | solution.py:119
  7.9 86.6 %all-gather.9.cloned.1.call-start = ((), (), s32[]{:S(2)}) async-start(), calls=%async_computation.6 | async-start | bytes 1179648 | tf_op jit(solution)/shard_map/all_gather | solution.py:69
  49.4 1.9 copy-start.2
  51.4 2.4 %copy-start.9 = (bf16[1536,128]{1,0:T(8,128)(2,1)S(1)}, bf16[1536,128]{1,0:T(8,128)(2,1)}, u32[]{:S(2)}) copy-start(bf16[1536,128]{1,0:T(8,128)(2,1)} %param.17) | copy-start | bytes 1179652
  51.4 2.4 %copy-start.10 = (f32[1536]{0:T(1024)S(1)}, f32[1536]{0:T(1024)}, u32[]{:S(2)}) copy-start(f32[1536]{0:T(1024)} %param.14) | copy-start | bytes 18436
  53.6 7.5 %copy-start.11 = (f32[12]{0:T(128)S(1)}, f32[12]{0:T(128)}, u32[]{:S(2)}) copy-start(f32[12]{0:T(128)} %param.19) | copy-start | bytes 148
  53.7 83.2 %reduce-scatter.3.cloned.1.call-start = ((), (), s32[]{:S(2)}) async-start(), calls=%async_computation.3 | async-start | bytes 1966080 | tf_op jit(solution)/shard_map/reduce_scatter | solution.py:133
  55.8 5.4 %copy-start.4 = (bf16[4,128,128]{2,1,0:T(8,128)(2,1)}, bf16[4,128,128]{2,1,0:T(8,128)(2,1)S(1)}, u32[]{:S(2)}) copy-start(bf16[4,128,128]{2,1,0:T(8,128)(2,1)S(1)} %convolution_convert_fusion) | copy-start | bytes 393220
  55.8 5.3 %collective-permute-start = (bf16[4,128,1,128]{3,1,0,2:T(8,128)(2,1)S(1)}, bf16[4,128,1,128]{3,1,0,2:T(8,128)(2,1)S(1)}, u32[]{:S(2)}, u32[]{:S(2)}) collective-permute-start(bf16[4,128,1,128]{3,1,0,2:T(8,128)(2,1)S(1)} %bitcast.105), channel_id=1, source_target_pairs={{0,4},{4,8},{8,12},{12,16},{16,20},{20,24},{24,28},{28,0},{1,5},{5... | collective-permute-start | bytes 393224 | tf_op jit(solution)/shard_map/ppermute | solution.py:20
  61.1 5.3 %collective-permute-start.1 = (bf16[4,128,1,128]{3,1,0,2:T(8,128)(2,1)S(1)}, bf16[4,128,1,128]{3,1,0,2:T(8,128)(2,1)S(1)}, u32[]{:S(2)}, u32[]{:S(2)}) collective-permute-start(bf16[4,128,1,128]{3,1,0,2:T(8,128)(2,1)S(1)} %collective-permute-done), channel_id=1, source_target_pairs={{0,4},{4,8},{8,12},{12,16},{16,20},{20,24},{24,28},{28,0},{1,5},{5... | collective-permute-start | bytes 393224 | tf_op jit(solution)/shard_map/ppermute | solution.py:20
  66.4 5.4 %collective-permute-start.2 = (bf16[4,128,1,128]{3,1,0,2:T(8,128)(2,1)S(1)}, bf16[4,128,1,128]{3,1,0,2:T(8,128)(2,1)}, u32[]{:S(2)}, u32[]{:S(2)}) collective-permute-start(bf16[4,128,1,128]{3,1,0,2:T(8,128)(2,1)S(1)} %collective-permute-done.1), channel_id=1, source_target_pairs={{0,4},{4,8},{8,12},{12,16},{16,20},{20,24},{24,28},{28,0},{1,5},{5... | collective-permute-start | bytes 393224 | tf_op jit(solution)/shard_map/ppermute | solution.py:20
  71.8 5.7 %collective-permute-start.3 = (bf16[4,128,1,128]{3,1,0,2:T(8,128)(2,1)}, bf16[4,128,1,128]{3,1,0,2:T(8,128)(2,1)}, u32[]{:S(2)}, u32[]{:S(2)}) collective-permute-start(bf16[4,128,1,128]{3,1,0,2:T(8,128)(2,1)} %collective-permute-done.2), channel_id=1, source_target_pairs={{0,4},{4,8},{8,12},{12,16},{16,20},{20,24},{24,28},{28,0},{1,5},{5... | collective-permute-start | bytes 393224 | tf_op jit(solution)/shard_map/ppermute | solution.py:20
  77.6 5.5 %collective-permute-start.4 = (bf16[4,128,1,128]{3,1,0,2:T(8,128)(2,1)}, bf16[4,128,1,128]{3,1,0,2:T(8,128)(2,1)S(1)}, u32[]{:S(2)}, u32[]{:S(2)}) collective-permute-start(bf16[4,128,1,128]{3,1,0,2:T(8,128)(2,1)} %collective-permute-done.3), channel_id=1, source_target_pairs={{0,4},{4,8},{8,12},{12,16},{16,20},{20,24},{24,28},{28,0},{1,5},{5... | collective-permute-start | bytes 393224 | tf_op jit(solution)/shard_map/ppermute | solution.py:20
  83.1 5.3 %collective-permute-start.5 = (bf16[4,128,1,128]{3,1,0,2:T(8,128)(2,1)S(1)}, bf16[4,128,1,128]{3,1,0,2:T(8,128)(2,1)S(1)}, u32[]{:S(2)}, u32[]{:S(2)}) collective-permute-start(bf16[4,128,1,128]{3,1,0,2:T(8,128)(2,1)S(1)} %collective-permute-done.4), channel_id=1, source_target_pairs={{0,4},{4,8},{8,12},{12,16},{16,20},{20,24},{24,28},{28,0},{1,5},{5... | collective-permute-start | bytes 393224 | tf_op jit(solution)/shard_map/ppermute | solution.py:20
  88.4 5.3 %collective-permute-start.6 = (bf16[4,128,1,128]{3,1,0,2:T(8,128)(2,1)S(1)}, bf16[4,128,1,128]{3,1,0,2:T(8,128)(2,1)S(1)}, u32[]{:S(2)}, u32[]{:S(2)}) collective-permute-start(bf16[4,128,1,128]{3,1,0,2:T(8,128)(2,1)S(1)} %collective-permute-done.5), channel_id=1, source_target_pairs={{0,4},{4,8},{8,12},{12,16},{16,20},{20,24},{24,28},{28,0},{1,5},{5... | collective-permute-start | bytes 393224 | tf_op jit(solution)/shard_map/ppermute | solution.py:20
  97.3 2.8 %copy-start.3 = (bf16[384,1536]{1,0:T(8,128)(2,1)S(1)}, bf16[384,1536]{1,0:T(8,128)(2,1)}, u32[]{:S(2)}) copy-start(bf16[384,1536]{1,0:T(8,128)(2,1)} %param.18) | copy-start | bytes 3538948
  102.3 34.6 %copy-start.1 = (bf16[1,128,1536]{2,1,0:T(8,128)(2,1)S(1)}, bf16[1,128,1536]{2,1,0:T(8,128)(2,1)}, u32[]{:S(2)}) copy-start(bf16[1,128,1536]{2,1,0:T(8,128)(2,1)} %param.13) | copy-start | bytes 1179652
  102.3 35.8 %copy-start.5 = (f32[1536]{0:T(1024)S(1)}, f32[1536]{0:T(1024)}, u32[]{:S(2)}) copy-start(f32[1536]{0:T(1024)} %param.20) | copy-start | bytes 18436
  102.3 37.9 %copy-start.6 = (s32[4,128,2]{1,2,0:T(2,128)S(1)}, s32[4,128,2]{1,2,0:T(2,128)}, u32[]{:S(2)}) copy-start(s32[4,128,2]{1,2,0:T(2,128)} %param.24) | copy-start | bytes 12292
  102.4 37.9 %copy-start.7 = (f32[4,128,2]{1,2,0:T(2,128)S(1)}, f32[4,128,2]{1,2,0:T(2,128)}, u32[]{:S(2)}) copy-start(f32[4,128,2]{1,2,0:T(2,128)} %param.25) | copy-start | bytes 12292
  102.4 73.9 %all-gather.7.cloned.1.call-start = ((), (), s32[]{:S(2)}) async-start(), calls=%async_computation.4 | async-start | bytes 1966080 | tf_op jit(solution)/shard_map/all_gather | solution.py:142
  140.0 82.1 %reduce-scatter.5.cloned.1.call-start = ((), (), s32[]{:S(2)}) async-start(), calls=%async_computation.5 | async-start | bytes 1966080 | tf_op jit(solution)/shard_map/reduce_scatter | solution.py:151
Sparse Core Ops, SparseCore 0:
  9.6 39.7 all-gather.4
  53.8 23.0 all-gather.8
  102.5 34.3 reduce-scatter.2
  140.2 36.0 all-gather.6
  188.0 34.1 reduce-scatter.4
